TPU v7x, 512 devices: a whole 4x4x16 slice. The times are simulated.
512 devices in a mesh: gz: 64 (over y, z), xy: 8 (over x, core).
Axes of the slice: x: 4, y: 4, z: 16, core: 2. Of those that a mesh axis runs over, the one named last changes fastest.
Arguments:
- right_side: float32 [2, 64, 64, 2048], P(None, 'gz', 'xy')
- stiff_across: float32 [64, 64, 2048], P('gz', 'xy'), may hold values from 0.3 to 3
- stiff_down: float32 [64, 64, 2048], P('gz', 'xy'), may hold values from 0.3 to 3
- anchor: float32 [64, 64, 2048], P('gz', 'xy'), may hold values from 0.02 to 0.2
- source_node: int32 [64, 8, 1024], P('gz', 'xy'), may hold values from 0 to 16383
- target_cell: int32 [64, 8, 1024], P('gz', 'xy'), may hold values from 0 to 14334, as said below
- corner_weight: float32 [4, 64, 8, 1024], P(None, 'gz', 'xy'), may hold values from 0 to 1, as said below
- block_count: int32 [64, 8], P('gz', 'xy'), may hold values from 1 to 8, as said below
Outputs:
- solution_field: float32 [2, 64, 64, 2048], P(None, 'gz', 'xy')
- residual: float32 [2, 64, 64, 2048], P(None, 'gz', 'xy')
Inputs may be any that keep to these rules, and one draw needn't show every extreme that they name: `target_cell`: each target cell's row is below 7 and its column below 2047 within the block, so all four corners lie in the same block. `corner_weight`: the weights of a slot are nonnegative and sum to 1. `block_count`: some device holds exactly 8 used blocks.
All inputs are finite; a program needn't handle non-finite values.
Results may differ from a plain program's by a relative error of at most 0.00013.
Values sent between devices are 32-bit elements; how exact they have to be, the bound alone decides.
A program may use at most 64 MiB of HBM per device.

v0:
```python
import jax
import jax.numpy as jnp
from jax import lax
from jax.sharding import Mesh
from jax.sharding import PartitionSpec as P

BLOCK = 128
ITERS = 3
GZ_XY = ("gz_0", "gz_1", "xy_0", "xy_1")
GZ = ("gz_0", "gz_1")
XY = ("xy_0", "xy_1")


def one_axis_at_a_time(shard, axes):
    for axis in axes:
        shard = lax.psum(shard, axis)
    return shard


def passed_along(block, axis, distance):
    devices = range(lax.axis_size(axis))
    route = [(i - distance, i) for i in devices if i - distance in devices]
    return lax.ppermute(block, axis, route)


def padded_2(cells, sides, width):
    for axis, dim in sides:
        count = lax.axis_size(axis)
        ends = count - 1
        head = lax.slice_in_dim(cells, 0, width, axis=dim)
        tail = lax.slice_in_dim(cells, cells.shape[dim] - width, cells.shape[dim], axis=dim)
        cells = jnp.concatenate(
            [
                lax.ppermute(tail, axis, [(i, (i + 1) % count) for i in range(ends)]),
                cells,
                lax.ppermute(head, axis, [((i + 1) % count, i) for i in range(ends)]),
            ],
            axis=dim,
        )
    return cells


def two_products(residual, image):
    return (
        one_axis_at_a_time(jnp.sum(residual * residual), GZ_XY),
        one_axis_at_a_time(jnp.sum(residual * image), GZ_XY),
    )


def body(
    right_side,
    stiff_across,
    stiff_down,
    anchor,
    source_node,
    target_cell,
    corner_weight,
    block_count,
):
    rows = stiff_across.shape[1]
    cols = stiff_across.shape[2]
    rhs = right_side[:, 0]
    across = stiff_across[0]
    down = stiff_down[0]
    hold = anchor[0]
    source = source_node[0, 0]
    target = target_cell[0, 0]
    weights = corner_weight[:, 0, 0]
    count = block_count[0, 0]
    slots = source.shape[0]
    has_next = lax.axis_index(GZ) < lax.axis_size(GZ) - 1
    live = ((jnp.arange(slots, dtype=jnp.int32) < count * BLOCK) & has_next).astype(jnp.float32)
    offsets = jnp.array([0, 1, cols, cols + 1], dtype=jnp.int32)
    corners = target[None, :] + offsets[:, None]
    rim = passed_along(down[-1:, :], XY, 1)
    down_above = jnp.concatenate([rim, down[:-1]], 0)
    across_left = jnp.concatenate([jnp.zeros((rows, 1), jnp.float32), across[:, :-1]], 1)
    got_corners = passed_along(corners, GZ, 1)
    got_weights = passed_along(weights, GZ, 1)

    def springs(field):
        padded = padded_2(field, ((XY, 1),), 1)
        upper = padded[:, :-2]
        lower = padded[:, 2:]
        zero_col = jnp.zeros((2, rows, 1), jnp.float32)
        right = jnp.concatenate([field[:, :, 1:], zero_col], 2)
        left = jnp.concatenate([zero_col, field[:, :, :-1]], 2)
        return (
            across * (field - right)
            + across_left * (field - left)
            + down * (field - lower)
            + down_above * (field - upper)
            + hold * field
        )

    def links(field):
        flat = field.reshape(2, rows * cols)
        own_values = flat[:, source]
        empty = jnp.zeros((2, rows * cols), jnp.float32)
        interp_mine = jnp.sum(got_weights[None] * flat[:, got_corners], 1)
        interp = passed_along(interp_mine, GZ, -1)
        error = (interp - own_values) * live[None]
        error_in = passed_along(error, GZ, 1)
        onward = empty.at[:, got_corners.reshape(-1)].add(
            (got_weights[None] * error_in[:, None, :]).reshape(2, -1)
        )
        own = empty.at[:, source].add(-error)
        return (own + onward).reshape(2, rows, cols)

    def operate(field):
        return springs(field) + links(field)

    solution_field = jnp.zeros_like(rhs)
    residual = rhs
    image = operate(residual)
    norm_now, product = two_products(residual, image)
    alpha = norm_now / product
    direction, along = (residual, image)
    for step in range(ITERS):
        solution_field = solution_field + alpha * direction
        residual = residual - alpha * along
        if step + 1 < ITERS:
            image = operate(residual)
            norm_next, product = two_products(residual, image)
            ratio = norm_next / norm_now
            alpha = norm_next / (product - ratio * norm_next / alpha)
            direction = residual + ratio * direction
            along = image + ratio * along
            norm_now = norm_next
    return (solution_field[:, None], residual[:, None])


def solution(mesh):
    split = Mesh(mesh.devices.reshape(4, 16, 4, 2), ("gz_0", "gz_1", "xy_0", "xy_1"))
    in_specs = (
        P(None, GZ, XY, None),
        P(GZ, XY, None),
        P(GZ, XY, None),
        P(GZ, XY, None),
        P(GZ, XY, None),
        P(GZ, XY, None),
        P(None, GZ, XY, None),
        P(GZ, XY),
    )
    out_specs = (P(None, GZ, XY, None), P(None, GZ, XY, None))
    return jax.shard_map(body, mesh=split, in_specs=in_specs, out_specs=out_specs, check_vma=False)
```

profile of v0, /device:TPU:1, one launch (start us, length us, event | category | flops | bytes accessed | tf_op | source)
XLA Modules:
  0.0 437.8 jit_solution(2395866498176098867)
XLA Ops:
  0.6 0.8 broadcast_add_fusion
  1.4 4.4 collective-permute-start.3
  5.8 0.7 copy.77
  6.5 3.5 collective-permute-start.4
  10.0 1.0 fusion.50
  11.1 3.5 collective-permute-start
  14.5 2.7 collective-permute-start.2
  17.2 0.9 slice_bitcast_fusion.1
  18.1 2.4 collective-permute-start.1
  20.5 1.1 fusion.49
  21.6 0.8 slice_bitcast_fusion
  23.8 5.5 %copy.51 = f32[2,1,8,2048]{0,3,2,1:T(8,128)} copy(f32[2,1,8,2048]{3,2,1,0:T(8,128)} %param.9) | data formatting | bytes 262144 | tf_op args[0]
  29.3 6.2 %gather_fusion.1 = f32[1024,2]{1,0:T(8,128)S(1)} fusion(f32[2,16384]{0,1:T(8,128)} %bitcast.83, s32[1024]{0:T(1024)S(1)} %broadcast_clamp_fusion), kind=kCustom, calls=%fused_computation.1 | custom fusion | bytes 20480 | tf_op jit(solution)/shard_map/gather | solution.py:98
  35.8 14.1 %gather_fusion = f32[4096,2]{1,0:T(8,128)S(1)} fusion(f32[2,16384]{0,1:T(8,128)} %bitcast.84, s32[4096]{0:T(1024)S(1)} %bitcast_clamp_fusion), kind=kCustom, calls=%fused_computation | custom fusion | bytes 81920 | tf_op jit(solution)/shard_map/gather | solution.py:100
  50.0 0.7 multiply_reduce_fusion.2
  50.9 1.3 collective-permute-start.5
  52.3 3.2 collective-permute-done.5
  55.5 4.8 %collective-permute-start.6 = (f32[2,1024]{1,0:T(2,128)S(1)}, f32[2,1024]{1,0:T(2,128)S(1)}, u32[]{:S(2)}, u32[]{:S(2)}) collective-permute-start(f32[2,1024]{1,0:T(2,128)S(1)} %get-tuple-element.40), channel_id=1, source_target_pairs={{0,8},{8,16},{16,24},{24,32},{32,40},{40,48},{48,56},{56,64},{64,7... | collective-permute-start | bytes 24584 | tf_op jit(solution)/shard_map/ppermute | solution.py:23
  60.3 0.7 collective-permute-done.6
  61.2 0.8 copy.54
  62.0 38.0 %scatter_custom_fusion = f32[2,16384]{0,1:T(8,128)} fusion(s32[5120]{0:T(1024)S(1)} %bitcast.115, f32[5120,2]{1,0:T(8,128)S(1)} %copy.54, f32[]{:T(128)} %constant.10.clone.1), kind=kCustom, calls=%fused_computation.13 | custom fusion | flops 10240 | bytes 131076 | tf_op jit(solution)/shard_map/add | solution.py:108
  100.0 5.3 %copy.55 = f32[2,8,2048]{2,1,0:T(8,128)S(1)} copy(f32[2,8,2048]{0,2,1:T(8,128)} %bitcast.81) | data formatting | bytes 262144 | tf_op jit(solution)/shard_map/reshape | solution.py:108
  105.3 0.7 multiply_reduce_fusion.7
  106.0 8.1 %all-reduce.15 = (f32[]{:T(128)}, f32[]{:T(128)}) all-reduce(f32[]{:T(128)} %get-tuple-element.7, f32[]{:T(128)} %get-tuple-element.6), channel_id=1, replica_groups=mesh['gz_0'=4,'gz_1'=16,'xy_0'=4,'xy_1'=2] {'gz_0'}, use_global_device_ids=true, to_apply=%region_1.0 | all-reduce | flops 2 | bytes 16 | tf_op jit(solution)/shard_map/psum | solution.py:16
  114.1 21.8 %all-reduce.9 = (f32[]{:T(128)}, f32[]{:T(128)}) all-reduce(f32[]{:T(128)} %get-tuple-element.24, f32[]{:T(128)} %get-tuple-element.25), channel_id=1, replica_groups=mesh['gz_0'=4,'gz_1'=16,'xy_0'=4,'xy_1'=2] {'gz_1'}, use_global_device_ids=true, to_apply=%region_2.0 | all-reduce | flops 2 | bytes 16 | tf_op jit(solution)/shard_map/psum | solution.py:16
  135.9 7.8 %all-reduce.12 = (f32[]{:T(128)}, f32[]{:T(128)}) all-reduce(f32[]{:T(128)} %get-tuple-element.12, f32[]{:T(128)} %get-tuple-element.13), channel_id=1, replica_groups=mesh['gz_0'=4,'gz_1'=16,'xy_0'=4,'xy_1'=2] {'xy_0'}, use_global_device_ids=true, to_apply=%region_3.0 | all-reduce | flops 2 | bytes 16 | tf_op jit(solution)/shard_map/psum | solution.py:16
  143.8 16.2 %all-reduce.18 = (f32[]{:T(128)}, f32[]{:T(128)}) all-reduce(f32[]{:T(128)} %get-tuple-element.18, f32[]{:T(128)} %get-tuple-element.19), channel_id=1, replica_groups=mesh['gz_0'=4,'gz_1'=16,'xy_0'=4,'xy_1'=2] {'xy_1'}, use_global_device_ids=true, to_apply=%region_4.0 | all-reduce | flops 2 | bytes 16 | tf_op jit(solution)/shard_map/psum | solution.py:16
  161.4 4.6 %copy.56 = f32[2,8,2048]{0,2,1:T(8,128)} copy(f32[2,8,2048]{2,1,0:T(8,128)S(1)} %multiply_subtract_fusion.1) | data formatting | bytes 262144 | tf_op jit(solution)/shard_map/sub | solution.py:121
  165.9 14.1 %gather_fusion.2 = f32[4096,2]{1,0:T(8,128)S(1)} fusion(f32[2,16384]{0,1:T(8,128)} %bitcast.87, s32[4096]{0:T(1024)S(1)} %bitcast_clamp_fusion), kind=kCustom, calls=%fused_computation.2 | custom fusion | bytes 81920 | tf_op jit(solution)/shard_map/gather | solution.py:100
  180.1 0.7 multiply_reduce_fusion.1
  181.0 1.3 collective-permute-start.9
  182.3 0.8 fusion.47
  183.1 6.2 %gather_fusion.3 = f32[1024,2]{1,0:T(8,128)S(1)} fusion(f32[2,16384]{0,1:T(8,128)} %bitcast.88, s32[1024]{0:T(1024)S(1)} %copy-done.13), kind=kCustom, calls=%fused_computation.3 | custom fusion | bytes 20480 | tf_op jit(solution)/shard_map/gather | solution.py:98
  189.5 4.0 collective-permute-start.10
  193.5 2.8 collective-permute-start.7
  196.3 2.8 collective-permute-start.8
  199.2 0.8 copy.59
  200.0 38.1 %scatter_custom_fusion.1 = f32[2,16384]{0,1:T(8,128)} fusion(s32[5120]{0:T(1024)} %bitcast.116, f32[5120,2]{1,0:T(8,128)S(1)} %copy.59, f32[]{:T(128)} %constant.10.clone.1), kind=kCustom, calls=%fused_computation.11 | custom fusion | flops 10240 | bytes 131584 | tf_op jit(solution)/shard_map/add | solution.py:108
  238.1 5.3 %copy.60 = f32[2,8,2048]{2,1,0:T(8,128)S(1)} copy(f32[2,8,2048]{0,2,1:T(8,128)} %bitcast.82) | data formatting | bytes 262144 | tf_op jit(solution)/shard_map/reshape | solution.py:108
  244.0 1.5 multiply_reduce_fusion.5
  245.5 6.7 %all-reduce.14 = (f32[]{:T(128)}, f32[]{:T(128)}) all-reduce(f32[]{:T(128)} %get-tuple-element.5, f32[]{:T(128)} %get-tuple-element.4), channel_id=1, replica_groups=mesh['gz_0'=4,'gz_1'=16,'xy_0'=4,'xy_1'=2] {'gz_0'}, use_global_device_ids=true, to_apply=%region_13.0 | all-reduce | flops 2 | bytes 16 | tf_op jit(solution)/shard_map/psum | solution.py:16
  252.3 20.7 %all-reduce.8 = (f32[]{:T(128)}, f32[]{:T(128)}) all-reduce(f32[]{:T(128)} %get-tuple-element.22, f32[]{:T(128)} %get-tuple-element.23), channel_id=1, replica_groups=mesh['gz_0'=4,'gz_1'=16,'xy_0'=4,'xy_1'=2] {'gz_1'}, use_global_device_ids=true, to_apply=%region_14.0 | all-reduce | flops 2 | bytes 16 | tf_op jit(solution)/shard_map/psum | solution.py:16
  272.9 6.9 %all-reduce.11 = (f32[]{:T(128)}, f32[]{:T(128)}) all-reduce(f32[]{:T(128)} %get-tuple-element.10, f32[]{:T(128)} %get-tuple-element.11), channel_id=1, replica_groups=mesh['gz_0'=4,'gz_1'=16,'xy_0'=4,'xy_1'=2] {'xy_0'}, use_global_device_ids=true, to_apply=%region_15.0 | all-reduce | flops 2 | bytes 16 | tf_op jit(solution)/shard_map/psum | solution.py:16
  279.8 13.2 %all-reduce.17 = (f32[]{:T(128)}, f32[]{:T(128)}) all-reduce(f32[]{:T(128)} %get-tuple-element.16, f32[]{:T(128)} %get-tuple-element.17), channel_id=1, replica_groups=mesh['gz_0'=4,'gz_1'=16,'xy_0'=4,'xy_1'=2] {'xy_1'}, use_global_device_ids=true, to_apply=%region_16.0 | all-reduce | flops 2 | bytes 16 | tf_op jit(solution)/shard_map/psum | solution.py:16
  297.7 4.6 %copy.61 = f32[2,8,2048]{0,2,1:T(8,128)} copy(f32[2,8,2048]{2,1,0:T(8,128)S(1)} %multiply_subtract_fusion) | data formatting | bytes 262144 | tf_op jit(solution)/shard_map/sub | solution.py:121
  302.3 14.1 %gather_fusion.4 = f32[4096,2]{1,0:T(8,128)S(1)} fusion(f32[2,16384]{0,1:T(8,128)} %bitcast.85, s32[4096]{0:T(1024)S(1)} %bitcast_clamp_fusion), kind=kCustom, calls=%fused_computation.4 | custom fusion | bytes 81920 | tf_op jit(solution)/shard_map/gather | solution.py:100
  316.4 0.7 multiply_reduce_fusion
  317.3 1.3 collective-permute-start.13
  318.6 0.8 fusion.45
  319.4 6.7 %gather_fusion.5 = f32[1024,2]{1,0:T(8,128)S(1)} fusion(f32[2,16384]{0,1:T(8,128)} %bitcast.86, s32[1024]{0:T(1024)} %copy-done.12), kind=kCustom, calls=%fused_computation.5 | custom fusion | bytes 20480 | tf_op jit(solution)/shard_map/gather | solution.py:98
  326.3 0.7 fusion.37
  327.0 4.3 collective-permute-start.14
  331.9 2.5 collective-permute-start.11
  334.4 3.0 collective-permute-start.12
  337.5 0.7 broadcast_multiply_fusion
  338.9 1.5 copy.64
  340.4 38.1 %scatter_custom_fusion.2 = f32[2,16384]{0,1:T(8,128)} fusion(s32[5120]{0:T(1024)} %bitcast.117, f32[5120,2]{1,0:T(8,128)S(1)} %copy.64, f32[]{:T(128)} %constant.10.clone.1), kind=kCustom, calls=%fused_computation.9 | custom fusion | flops 10240 | bytes 131584 | tf_op jit(solution)/shard_map/add | solution.py:108
  378.5 5.3 %copy.65 = f32[2,8,2048]{2,1,0:T(8,128)S(1)} copy(f32[2,8,2048]{0,2,1:T(8,128)} %bitcast.80) | data formatting | bytes 262144 | tf_op jit(solution)/shard_map/reshape | solution.py:108
  383.9 1.5 multiply_reduce_fusion.3
  385.3 6.6 %all-reduce.13 = (f32[]{:T(128)}, f32[]{:T(128)}) all-reduce(f32[]{:T(128)} %get-tuple-element.3, f32[]{:T(128)} %get-tuple-element.2), channel_id=1, replica_groups=mesh['gz_0'=4,'gz_1'=16,'xy_0'=4,'xy_1'=2] {'gz_0'}, use_global_device_ids=true, to_apply=%region_25.0 | all-reduce | flops 2 | bytes 16 | tf_op jit(solution)/shard_map/psum | solution.py:16
  391.9 21.0 %all-reduce.7 = (f32[]{:T(128)}, f32[]{:T(128)}) all-reduce(f32[]{:T(128)} %get-tuple-element.20, f32[]{:T(128)} %get-tuple-element.21), channel_id=1, replica_groups=mesh['gz_0'=4,'gz_1'=16,'xy_0'=4,'xy_1'=2] {'gz_1'}, use_global_device_ids=true, to_apply=%region_26.0 | all-reduce | flops 2 | bytes 16 | tf_op jit(solution)/shard_map/psum | solution.py:16
  412.9 7.3 %all-reduce.10 = (f32[]{:T(128)}, f32[]{:T(128)}) all-reduce(f32[]{:T(128)} %get-tuple-element.8, f32[]{:T(128)} %get-tuple-element.9), channel_id=1, replica_groups=mesh['gz_0'=4,'gz_1'=16,'xy_0'=4,'xy_1'=2] {'xy_0'}, use_global_device_ids=true, to_apply=%region_27.0 | all-reduce | flops 2 | bytes 16 | tf_op jit(solution)/shard_map/psum | solution.py:16
  420.2 12.8 %all-reduce.16 = (f32[]{:T(128)}, f32[]{:T(128)}) all-reduce(f32[]{:T(128)} %get-tuple-element.14, f32[]{:T(128)} %get-tuple-element.15), channel_id=1, replica_groups=mesh['gz_0'=4,'gz_1'=16,'xy_0'=4,'xy_1'=2] {'xy_1'}, use_global_device_ids=true, to_apply=%region_28.0 | all-reduce | flops 2 | bytes 16 | tf_op jit(solution)/shard_map/psum | solution.py:16
  437.0 0.8 subtract_bitcast_fusion
  (81 shorter events, 4.2 us)
Async XLA Ops:
  1.4 34.4 %collective-permute-start.3 = (s32[4,1024]{1,0:T(4,128)S(1)}, s32[4,1024]{1,0:T(4,128)S(1)}, u32[]{:S(2)}, u32[]{:S(2)}) collective-permute-start(s32[4,1024]{1,0:T(4,128)S(1)} %broadcast_add_fusion), channel_id=1, source_target_pairs={{0,8},{8,16},{16,24},{24,32},{32,40},{40,48},{48,56},{56,64},{64,7... | collective-permute-start | bytes 49160 | tf_op jit(solution)/shard_map/ppermute | solution.py:23
  6.5 43.5 %collective-permute-start.4 = (f32[4,1024]{1,0:T(4,128)S(1)}, f32[4,1024]{1,0:T(4,128)S(1)}, u32[]{:S(2)}, u32[]{:S(2)}) collective-permute-start(f32[4,1024]{1,0:T(4,128)S(1)} %bitcast.118), channel_id=1, source_target_pairs={{0,8},{8,16},{16,24},{24,32},{32,40},{40,48},{48,56},{56,64},{64,7... | collective-permute-start | bytes 49160 | tf_op jit(solution)/shard_map/ppermute | solution.py:23
  11.1 94.2 %collective-permute-start = (f32[2,1,2048]{2,1,0:T(1,128)S(1)}, f32[2,1,2048]{2,1,0:T(1,128)S(1)}, u32[]{:S(2)}, u32[]{:S(2)}) collective-permute-start(f32[2,1,2048]{2,1,0:T(1,128)S(1)} %get-tuple-element.53), channel_id=1, source_target_pairs={{1,0},{2,1},{3,2},{4,3},{5,4},{6,5},{7,6},{9,8},{10,9},{11,10},{12... | collective-permute-start | bytes 49160 | tf_op jit(solution)/shard_map/ppermute | solution.py:36
  14.5 90.7 %collective-permute-start.2 = (f32[2,1,2048]{2,1,0:T(1,128)S(1)}, f32[2,1,2048]{2,1,0:T(1,128)S(1)}, u32[]{:S(2)}, u32[]{:S(2)}) collective-permute-start(f32[2,1,2048]{2,1,0:T(1,128)S(1)} %get-tuple-element.54), channel_id=1, source_target_pairs={{0,1},{1,2},{2,3},{3,4},{4,5},{5,6},{6,7},{8,9},{9,10},{10,11},{11... | collective-permute-start | bytes 49160 | tf_op jit(solution)/shard_map/ppermute | solution.py:34
  18.1 17.7 %collective-permute-start.1 = (f32[1,2048]{1,0:T(1,128)S(1)}, f32[1,2048]{1,0:T(1,128)S(1)}, u32[]{:S(2)}, u32[]{:S(2)}) collective-permute-start(f32[1,2048]{1,0:T(1,128)S(1)} %slice_bitcast_fusion.1), channel_id=1, source_target_pairs={{0,1},{1,2},{2,3},{3,4},{4,5},{5,6},{6,7},{8,9},{9,10},{10,11},{11... | collective-permute-start | bytes 24584 | tf_op jit(solution)/shard_map/ppermute | solution.py:23
  23.1 6.2 %copy-start.12 = (s32[1024]{0:T(1024)}, s32[1024]{0:T(1024)S(1)}, u32[]{:S(2)}) copy-start(s32[1024]{0:T(1024)S(1)} %broadcast_clamp_fusion) | copy-start | bytes 12292
  23.8 31.7 %copy-start.10 = (f32[1024]{0:T(1024)}, f32[1024]{0:T(1024)S(1)}, u32[]{:S(2)}) copy-start(f32[1024]{0:T(1024)S(1)} %fusion.35) | copy-start | bytes 12292
  23.8 11.9 %copy-start.2 = (f32[1,8,2048]{2,1,0:T(8,128)S(1)}, f32[1,8,2048]{2,1,0:T(8,128)}, u32[]{:S(2)}) copy-start(f32[1,8,2048]{2,1,0:T(8,128)} %param.10) | copy-start | bytes 196612
  50.9 4.6 %collective-permute-start.5 = (f32[2,1024]{1,0:T(2,128)S(1)}, f32[2,1024]{1,0:T(2,128)S(1)}, u32[]{:S(2)}, u32[]{:S(2)}) collective-permute-start(f32[2,1024]{1,0:T(2,128)S(1)} %bitcast.121), channel_id=1, source_target_pairs={{8,0},{16,8},{24,16},{32,24},{40,32},{48,40},{56,48},{64,56},{72,6... | collective-permute-start | bytes 24584 | tf_op jit(solution)/shard_map/ppermute | solution.py:23
  55.5 5.5 %collective-permute-start.6 = (f32[2,1024]{1,0:T(2,128)S(1)}, f32[2,1024]{1,0:T(2,128)S(1)}, u32[]{:S(2)}, u32[]{:S(2)}) collective-permute-start(f32[2,1024]{1,0:T(2,128)S(1)} %get-tuple-element.40), channel_id=1, source_target_pairs={{0,8},{8,16},{16,24},{24,32},{32,40},{40,48},{48,56},{56,64},{64,7... | collective-permute-start | bytes 24584 | tf_op jit(solution)/shard_map/ppermute | solution.py:23
  60.3 39.6 %copy-start.14 = (s32[5120,1]{0,1:T(1,128)}, s32[5120,1]{0,1:T(1,128)S(1)}, u32[]{:S(2)}) copy-start(s32[5120,1]{0,1:T(1,128)S(1)} %pad_add_fusion) | copy-start | bytes 61444
  60.3 138.8 %copy-start.9 = (f32[1,8,4,128]{3,1,2,0:T(8,128)}, f32[1,8,4,128]{3,1,2,0:T(8,128)S(1)}, u32[]{:S(2)}) copy-start(f32[1,8,4,128]{3,1,2,0:T(8,128)S(1)} %copy.76) | copy-start | bytes 49156
  100.0 5.3 %copy-start = (f32[2,1,8,2048]{3,2,1,0:T(8,128)S(1)}, f32[2,1,8,2048]{3,2,1,0:T(8,128)}, u32[]{:S(2)}) copy-start(f32[2,1,8,2048]{3,2,1,0:T(8,128)} %param.9) | copy-start | bytes 393220
  100.0 5.3 %copy-start.1 = (f32[1,8,2048]{2,1,0:T(8,128)S(1)}, f32[1,8,2048]{2,1,0:T(8,128)}, u32[]{:S(2)}) copy-start(f32[1,8,2048]{2,1,0:T(8,128)} %param.11) | copy-start | bytes 196612
  100.0 5.3 %copy-start.3 = (f32[1,8,2048]{2,1,0:T(8,128)S(1)}, f32[1,8,2048]{2,1,0:T(8,128)}, u32[]{:S(2)}) copy-start(f32[1,8,2048]{2,1,0:T(8,128)} %param.12) | copy-start | bytes 196612
  165.9 17.1 %copy-start.13 = (s32[1024]{0:T(1024)S(1)}, s32[1024]{0:T(1024)}, u32[]{:S(2)}) copy-start(s32[1024]{0:T(1024)} %copy-done.12) | copy-start | bytes 12292
  165.9 23.5 %copy-start.11 = (f32[1024]{0:T(1024)S(1)}, f32[1024]{0:T(1024)}, u32[]{:S(2)}) copy-start(f32[1024]{0:T(1024)} %copy-done.10) | copy-start | bytes 12292
  181.0 8.4 %collective-permute-start.9 = (f32[2,1024]{1,0:T(2,128)S(1)}, f32[2,1024]{1,0:T(2,128)S(1)}, u32[]{:S(2)}, u32[]{:S(2)}) collective-permute-start(f32[2,1024]{1,0:T(2,128)S(1)} %bitcast.120), channel_id=1, source_target_pairs={{8,0},{16,8},{24,16},{32,24},{40,32},{48,40},{56,48},{64,56},{72,6... | collective-permute-start | bytes 24584 | tf_op jit(solution)/shard_map/ppermute | solution.py:23
  189.5 9.6 %collective-permute-start.10 = (f32[2,1024]{1,0:T(2,128)S(1)}, f32[2,1024]{1,0:T(2,128)S(1)}, u32[]{:S(2)}, u32[]{:S(2)}) collective-permute-start(f32[2,1024]{1,0:T(2,128)S(1)} %get-tuple-element.37), channel_id=1, source_target_pairs={{0,8},{8,16},{16,24},{24,32},{32,40},{40,48},{48,56},{56,64},{64,7... | collective-permute-start | bytes 24584 | tf_op jit(solution)/shard_map/ppermute | solution.py:23
  193.5 49.9 %collective-permute-start.7 = (f32[2,1,2048]{2,1,0:T(1,128)S(1)}, f32[2,1,2048]{2,1,0:T(1,128)S(1)}, u32[]{:S(2)}, u32[]{:S(2)}) collective-permute-start(f32[2,1,2048]{2,1,0:T(1,128)S(1)} %get-tuple-element.49), channel_id=1, source_target_pairs={{1,0},{2,1},{3,2},{4,3},{5,4},{6,5},{7,6},{9,8},{10,9},{11,10},{12... | collective-permute-start | bytes 49160 | tf_op jit(solution)/shard_map/ppermute | solution.py:36
  196.3 47.1 %collective-permute-start.8 = (f32[2,1,2048]{2,1,0:T(1,128)S(1)}, f32[2,1,2048]{2,1,0:T(1,128)S(1)}, u32[]{:S(2)}, u32[]{:S(2)}) collective-permute-start(f32[2,1,2048]{2,1,0:T(1,128)S(1)} %get-tuple-element.50), channel_id=1, source_target_pairs={{0,1},{1,2},{2,3},{3,4},{4,5},{5,6},{6,7},{8,9},{9,10},{10,11},{11... | collective-permute-start | bytes 49160 | tf_op jit(solution)/shard_map/ppermute | solution.py:34
  238.1 5.9 %copy-start.7 = (f32[2,8,2047]{2,1,0:T(8,128)S(1)}, f32[2,8,2047]{2,1,0:T(8,128)}, u32[]{:S(2)}) copy-start(f32[2,8,2047]{2,1,0:T(8,128)} %get-tuple-element.47) | copy-start | bytes 393028
  238.1 5.9 %copy-start.8 = (f32[2,8,2047]{2,1,0:T(8,128)S(1)}, f32[2,8,2047]{2,1,0:T(8,128)}, u32[]{:S(2)}) copy-start(f32[2,8,2047]{2,1,0:T(8,128)} %get-tuple-element.48) | copy-start | bytes 393028
  243.4 0.6 copy-start.15
  243.4 0.6 copy-start.16
  317.3 8.9 %collective-permute-start.13 = (f32[2,1024]{1,0:T(2,128)S(1)}, f32[2,1024]{1,0:T(2,128)S(1)}, u32[]{:S(2)}, u32[]{:S(2)}) collective-permute-start(f32[2,1024]{1,0:T(2,128)S(1)} %bitcast.119), channel_id=1, source_target_pairs={{8,0},{16,8},{24,16},{32,24},{40,32},{48,40},{56,48},{64,56},{72,6... | collective-permute-start | bytes 24584 | tf_op jit(solution)/shard_map/ppermute | solution.py:23
  327.0 10.5 %collective-permute-start.14 = (f32[2,1024]{1,0:T(2,128)S(1)}, f32[2,1024]{1,0:T(2,128)S(1)}, u32[]{:S(2)}, u32[]{:S(2)}) collective-permute-start(f32[2,1024]{1,0:T(2,128)S(1)} %get-tuple-element.34), channel_id=1, source_target_pairs={{0,8},{8,16},{16,24},{24,32},{32,40},{40,48},{48,56},{56,64},{64,7... | collective-permute-start | bytes 24584 | tf_op jit(solution)/shard_map/ppermute | solution.py:23
  331.9 51.9 %collective-permute-start.11 = (f32[2,1,2048]{2,1,0:T(1,128)}, f32[2,1,2048]{2,1,0:T(1,128)S(1)}, u32[]{:S(2)}, u32[]{:S(2)}) collective-permute-start(f32[2,1,2048]{2,1,0:T(1,128)} %get-tuple-element.45), channel_id=1, source_target_pairs={{1,0},{2,1},{3,2},{4,3},{5,4},{6,5},{7,6},{9,8},{10,9},{11,10},{12... | collective-permute-start | bytes 49160 | tf_op jit(solution)/shard_map/ppermute | solution.py:36
  334.4 49.4 %collective-permute-start.12 = (f32[2,1,2048]{2,1,0:T(1,128)}, f32[2,1,2048]{2,1,0:T(1,128)}, u32[]{:S(2)}, u32[]{:S(2)}) collective-permute-start(f32[2,1,2048]{2,1,0:T(1,128)} %get-tuple-element.46), channel_id=1, source_target_pairs={{0,1},{1,2},{2,3},{3,4},{4,5},{5,6},{6,7},{8,9},{9,10},{10,11},{11... | collective-permute-start | bytes 49160 | tf_op jit(solution)/shard_map/ppermute | solution.py:34
  378.5 5.3 %copy-start.4 = (f32[1,8,2048]{2,1,0:T(8,128)S(1)}, f32[1,8,2048]{2,1,0:T(8,128)}, u32[]{:S(2)}) copy-start(f32[1,8,2048]{2,1,0:T(8,128)} %param.12) | copy-start | bytes 196612
  378.5 5.3 %copy-start.5 = (f32[2,8,2047]{2,1,0:T(8,128)S(1)}, f32[2,8,2047]{2,1,0:T(8,128)}, u32[]{:S(2)}) copy-start(f32[2,8,2047]{2,1,0:T(8,128)} %get-tuple-element.43) | copy-start | bytes 393028
  378.5 5.3 %copy-start.6 = (f32[2,8,2047]{2,1,0:T(8,128)S(1)}, f32[2,8,2047]{2,1,0:T(8,128)}, u32[]{:S(2)}) copy-start(f32[2,8,2047]{2,1,0:T(8,128)} %get-tuple-element.44) | copy-start | bytes 393028
where the time goes:
time: 440 us; the launch traced here: 438 us
  blocking collectives  149 us (34%)
  other arithmetic  125 us (28%)
  local copies, waits for them, and re-layouts  104 us (24%)
  starting transfers between devices  44.4 us (10%)
  between operations  11.8 us (3%)
    psum x12, blocking collectives, one_axis_at_a_time(): shard = lax.psum(shard, axis)  149 us
    add x3, other arithmetic, links(): return (own + onward).reshape(2, rows, cols)  114 us
    gather x3, local copies, waits for them, and re-layouts, links(): interp_mine = jnp.sum(got_weights[None] * flat[:, got_corners], 1)  42.4 us
    ppermute x9, starting transfers between devices, passed_along(): return lax.ppermute(block, axis, route)  27.2 us
    gather x6, local copies, waits for them, and re-layouts, links(): own_values = flat[:, source]  19.6 us
    reshape x3, local copies, waits for them, and re-layouts, links(): return (own + onward).reshape(2, rows, cols)  15.8 us
    sub x2, local copies, waits for them, and re-layouts, body(): residual = residual - alpha * along  9.15 us
  transfers between devices with their start and end apart: 15, of which 2 were waited for; matrix products, arithmetic and copies ran while one was open for 42% of the time, Pallas kernels for 0%

commit v1 on v0

--- a/solution.py
+++ b/solution.py
@@ -13,7 +13,8 @@
 
 def one_axis_at_a_time(shard, axes):
     for axis in axes:
-        shard = lax.psum(shard, axis)
+        parts = lax.all_gather(shard, axis)
+        shard = jnp.sum(parts, axis=0)
     return shard
 
 

time: 440 us -> 486 us (1.10)
  local copies, waits for them, and re-layouts: 104 us -> 142 us
  other arithmetic: 125 us -> 139 us
  blocking collectives: 149 us -> 141 us
    psum x12 -> x0, blocking collectives: 149 us -> none  [one_axis_at_a_time(): shard = lax.psum(shard, axis)]
    unnamed x0 -> x12, blocking collectives: none -> 141 us
    unnamed x44 -> x96, local copies, waits for them, and re-layouts: 6.98 us -> 45.7 us
    reduce_sum x0 -> x24, other arithmetic: none -> 14.6 us  [one_axis_at_a_time(): shard = jnp.sum(parts, axis=0)]
  transfers between devices with their start and end apart: 15 -> 15, of which waited for: 2 -> 2; matrix products, arithmetic and copies ran while one was open for 42% -> 38% of each run, Pallas kernels for 0% -> 0%
where the time goes in v1:
time: 486 us; the launch traced here: 484 us
  local copies, waits for them, and re-layouts  142 us (29%)
  blocking collectives  141 us (29%)
  other arithmetic  139 us (29%)
  starting transfers between devices  44.6 us (9%)
  between operations  12.1 us (2%)
    unnamed x12, blocking collectives  141 us
    add x3, other arithmetic, links(): return (own + onward).reshape(2, rows, cols)  114 us
    unnamed x96, local copies, waits for them, and re-layouts  45.7 us
    gather x3, local copies, waits for them, and re-layouts, links(): interp_mine = jnp.sum(got_weights[None] * flat[:, got_corners], 1)  42.4 us
    ppermute x9, starting transfers between devices, passed_along(): return lax.ppermute(block, axis, route)  27.2 us
    gather x6, local copies, waits for them, and re-layouts, links(): own_values = flat[:, source]  19.6 us
    reshape x3, local copies, waits for them, and re-layouts, links(): return (own + onward).reshape(2, rows, cols)  15.8 us
    reduce_sum x24, other arithmetic, one_axis_at_a_time(): shard = jnp.sum(parts, axis=0)  14.6 us
  transfers between devices with their start and end apart: 15, of which 2 were waited for; matrix products, arithmetic and copies ran while one was open for 38% of the time, Pallas kernels for 0%

profile of v1, /device:TPU:1, one launch (start us, length us, event | category | flops | bytes accessed | tf_op | source)
XLA Modules:
  0.0 483.8 jit_solution(16346929612817634782)
XLA Ops:
  1.4 4.4 collective-permute-start.3
  6.5 3.5 collective-permute-start.4
  11.1 3.5 collective-permute-start
  14.5 2.7 collective-permute-start.2
  18.1 2.4 collective-permute-start.1
  23.8 5.5 %copy.51 = f32[2,1,8,2048]{0,3,2,1:T(8,128)} copy(f32[2,1,8,2048]{3,2,1,0:T(8,128)} %param.9) | data formatting | bytes 262144 | tf_op args[0]
  29.3 6.2 %gather_fusion.1 = f32[1024,2]{1,0:T(8,128)S(1)} fusion(f32[2,16384]{0,1:T(8,128)} %bitcast.111, s32[1024]{0:T(1024)S(1)} %broadcast_clamp_fusion), kind=kCustom, calls=%fused_computation.1 | custom fusion | bytes 20480 | tf_op jit(solution)/shard_map/gather | solution.py:99
  38.5 14.1 %gather_fusion = f32[4096,2]{1,0:T(8,128)S(1)} fusion(f32[2,16384]{0,1:T(8,128)} %bitcast.112, s32[4096]{0:T(1024)S(1)} %bitcast_clamp_fusion), kind=kCustom, calls=%fused_computation | custom fusion | bytes 81920 | tf_op jit(solution)/shard_map/gather | solution.py:101
  54.9 3.2 collective-permute-done.5
  58.2 4.8 collective-permute-start.6
  64.6 38.0 %scatter_custom_fusion = f32[2,16384]{0,1:T(8,128)} fusion(s32[5120]{0:T(1024)S(1)} %bitcast.143, f32[5120,2]{1,0:T(8,128)S(1)} %copy.54, f32[]{:T(128)} %constant.10.clone.1), kind=kCustom, calls=%fused_computation.13 | custom fusion | flops 10240 | bytes 131076 | tf_op jit(solution)/shard_map/add | solution.py:109
  102.6 5.3 %copy.55 = f32[2,8,2048]{2,1,0:T(8,128)S(1)} copy(f32[2,8,2048]{0,2,1:T(8,128)} %bitcast.109) | data formatting | bytes 262144 | tf_op jit(solution)/shard_map/reshape | solution.py:109
  110.0 1.4 dynamic-update-slice.4
  112.7 7.4 %all-reduce.39 = (f32[4]{0:T(128)S(1)}, f32[4]{0:T(128)S(1)}) all-reduce(f32[4]{0:T(128)S(1)} %dynamic-update-slice, f32[4]{0:T(128)S(1)} %dynamic-update-slice.4), channel_id=1, replica_groups=mesh['gz_0'=4,'gz_1'=16,'xy_0'=4,'xy_1'=2] {'gz_0'}, use_global_device_ids=true, to_apply=%add.7 | all-reduce | flops 8 | bytes 64
  121.4 1.4 dynamic-update-slice.5
  122.8 1.4 dynamic-update-slice.1
  124.1 21.2 %all-reduce.33 = (f32[16]{0:T(128)S(1)}, f32[16]{0:T(128)S(1)}) all-reduce(f32[16]{0:T(128)S(1)} %dynamic-update-slice.1, f32[16]{0:T(128)S(1)} %dynamic-update-slice.5), channel_id=1, replica_groups=mesh['gz_0'=4,'gz_1'=16,'xy_0'=4,'xy_1'=2] {'gz_1'}, use_global_device_ids=true, to_apply=%add.8 | all-reduce | flops 32 | bytes 256
  146.6 1.4 dynamic-update-slice.6
  148.0 1.4 dynamic-update-slice.2
  150.7 7.2 %all-reduce.36 = (f32[4]{0:T(128)S(1)}, f32[4]{0:T(128)S(1)}) all-reduce(f32[4]{0:T(128)S(1)} %dynamic-update-slice.2, f32[4]{0:T(128)S(1)} %dynamic-update-slice.6), channel_id=1, replica_groups=mesh['gz_0'=4,'gz_1'=16,'xy_0'=4,'xy_1'=2] {'xy_0'}, use_global_device_ids=true, to_apply=%add.9 | all-reduce | flops 8 | bytes 64
  159.1 1.4 dynamic-update-slice.7
  160.5 1.4 dynamic-update-slice.3
  161.9 15.5 %all-reduce.42 = (f32[2]{0:T(128)S(1)}, f32[2]{0:T(128)S(1)}) all-reduce(f32[2]{0:T(128)S(1)} %dynamic-update-slice.3, f32[2]{0:T(128)S(1)} %dynamic-update-slice.7), channel_id=1, replica_groups=mesh['gz_0'=4,'gz_1'=16,'xy_0'=4,'xy_1'=2] {'xy_1'}, use_global_device_ids=true, to_apply=%add.10 | all-reduce | flops 4 | bytes 32
  180.1 4.6 copy.56
  184.7 14.1 %gather_fusion.2 = f32[4096,2]{1,0:T(8,128)S(1)} fusion(f32[2,16384]{0,1:T(8,128)} %bitcast.115, s32[4096]{0:T(1024)S(1)} %bitcast_clamp_fusion), kind=kCustom, calls=%fused_computation.2 | custom fusion | bytes 81920 | tf_op jit(solution)/shard_map/gather | solution.py:101
  201.8 6.2 %gather_fusion.3 = f32[1024,2]{1,0:T(8,128)S(1)} fusion(f32[2,16384]{0,1:T(8,128)} %bitcast.116, s32[1024]{0:T(1024)S(1)} %copy-done.13), kind=kCustom, calls=%fused_computation.3 | custom fusion | bytes 20480 | tf_op jit(solution)/shard_map/gather | solution.py:99
  208.2 4.0 collective-permute-start.10
  212.2 2.8 collective-permute-start.7
  215.0 2.9 collective-permute-start.8
  218.9 38.1 %scatter_custom_fusion.1 = f32[2,16384]{0,1:T(8,128)} fusion(s32[5120]{0:T(1024)} %bitcast.144, f32[5120,2]{1,0:T(8,128)S(1)} %copy.59, f32[]{:T(128)} %constant.10.clone.1), kind=kCustom, calls=%fused_computation.11 | custom fusion | flops 10240 | bytes 131584 | tf_op jit(solution)/shard_map/add | solution.py:109
  257.0 5.3 %copy.60 = f32[2,8,2048]{2,1,0:T(8,128)S(1)} copy(f32[2,8,2048]{0,2,1:T(8,128)} %bitcast.110) | data formatting | bytes 262144 | tf_op jit(solution)/shard_map/reshape | solution.py:109
  262.9 1.5 multiply_reduce_fusion.5
  265.8 1.4 dynamic-update-slice.8
  267.2 6.1 %all-reduce.38 = (f32[4]{0:T(128)S(1)}, f32[4]{0:T(128)S(1)}) all-reduce(f32[4]{0:T(128)S(1)} %dynamic-update-slice.8, f32[4]{0:T(128)S(1)} %dynamic-update-slice.12), channel_id=1, replica_groups=mesh['gz_0'=4,'gz_1'=16,'xy_0'=4,'xy_1'=2] {'gz_0'}, use_global_device_ids=true, to_apply=%add.15 | all-reduce | flops 8 | bytes 64
  273.9 1.4 dynamic-update-slice.13
  275.9 1.4 dynamic-update-slice.9
  277.3 20.0 %all-reduce.32 = (f32[16]{0:T(128)S(1)}, f32[16]{0:T(128)S(1)}) all-reduce(f32[16]{0:T(128)S(1)} %dynamic-update-slice.9, f32[16]{0:T(128)S(1)} %dynamic-update-slice.13), channel_id=1, replica_groups=mesh['gz_0'=4,'gz_1'=16,'xy_0'=4,'xy_1'=2] {'gz_1'}, use_global_device_ids=true, to_apply=%add.16 | all-reduce | flops 32 | bytes 256
  297.9 1.4 dynamic-update-slice.14
  299.9 1.4 dynamic-update-slice.10
  301.4 6.3 %all-reduce.35 = (f32[4]{0:T(128)S(1)}, f32[4]{0:T(128)S(1)}) all-reduce(f32[4]{0:T(128)S(1)} %dynamic-update-slice.10, f32[4]{0:T(128)S(1)} %dynamic-update-slice.14), channel_id=1, replica_groups=mesh['gz_0'=4,'gz_1'=16,'xy_0'=4,'xy_1'=2] {'xy_0'}, use_global_device_ids=true, to_apply=%add.17 | all-reduce | flops 8 | bytes 64
  308.2 1.4 dynamic-update-slice.15
  310.2 1.4 dynamic-update-slice.11
  311.6 12.5 %all-reduce.41 = (f32[2]{0:T(128)S(1)}, f32[2]{0:T(128)S(1)}) all-reduce(f32[2]{0:T(128)S(1)} %dynamic-update-slice.11, f32[2]{0:T(128)S(1)} %dynamic-update-slice.15), channel_id=1, replica_groups=mesh['gz_0'=4,'gz_1'=16,'xy_0'=4,'xy_1'=2] {'xy_1'}, use_global_device_ids=true, to_apply=%add.18 | all-reduce | flops 4 | bytes 32
  330.2 4.6 copy.61
  334.8 14.1 %gather_fusion.4 = f32[4096,2]{1,0:T(8,128)S(1)} fusion(f32[2,16384]{0,1:T(8,128)} %bitcast.113, s32[4096]{0:T(1024)S(1)} %bitcast_clamp_fusion), kind=kCustom, calls=%fused_computation.4 | custom fusion | bytes 81920 | tf_op jit(solution)/shard_map/gather | solution.py:101
  351.9 6.7 %gather_fusion.5 = f32[1024,2]{1,0:T(8,128)S(1)} fusion(f32[2,16384]{0,1:T(8,128)} %bitcast.114, s32[1024]{0:T(1024)} %copy-done.12), kind=kCustom, calls=%fused_computation.5 | custom fusion | bytes 20480 | tf_op jit(solution)/shard_map/gather | solution.py:99
  359.5 4.3 collective-permute-start.14
  364.4 2.5 collective-permute-start.11
  366.9 3.0 collective-permute-start.12
  371.4 1.5 copy.64
  372.9 38.1 %scatter_custom_fusion.2 = f32[2,16384]{0,1:T(8,128)} fusion(s32[5120]{0:T(1024)} %bitcast.145, f32[5120,2]{1,0:T(8,128)S(1)} %copy.64, f32[]{:T(128)} %constant.10.clone.1), kind=kCustom, calls=%fused_computation.9 | custom fusion | flops 10240 | bytes 131584 | tf_op jit(solution)/shard_map/add | solution.py:109
  411.0 5.3 %copy.65 = f32[2,8,2048]{2,1,0:T(8,128)S(1)} copy(f32[2,8,2048]{0,2,1:T(8,128)} %bitcast.108) | data formatting | bytes 262144 | tf_op jit(solution)/shard_map/reshape | solution.py:109
  416.4 1.5 multiply_reduce_fusion.3
  419.2 1.4 dynamic-update-slice.16
  420.6 6.0 %all-reduce.37 = (f32[4]{0:T(128)S(1)}, f32[4]{0:T(128)S(1)}) all-reduce(f32[4]{0:T(128)S(1)} %dynamic-update-slice.16, f32[4]{0:T(128)S(1)} %dynamic-update-slice.20), channel_id=1, replica_groups=mesh['gz_0'=4,'gz_1'=16,'xy_0'=4,'xy_1'=2] {'gz_0'}, use_global_device_ids=true, to_apply=%add.23 | all-reduce | flops 8 | bytes 64
  427.2 1.4 dynamic-update-slice.21
  429.2 1.4 dynamic-update-slice.17
  430.5 20.3 %all-reduce.31 = (f32[16]{0:T(128)S(1)}, f32[16]{0:T(128)S(1)}) all-reduce(f32[16]{0:T(128)S(1)} %dynamic-update-slice.17, f32[16]{0:T(128)S(1)} %dynamic-update-slice.21), channel_id=1, replica_groups=mesh['gz_0'=4,'gz_1'=16,'xy_0'=4,'xy_1'=2] {'gz_1'}, use_global_device_ids=true, to_apply=%add.24 | all-reduce | flops 32 | bytes 256
  451.5 1.4 dynamic-update-slice.22
  453.5 1.4 dynamic-update-slice.18
  454.9 6.7 %all-reduce.34 = (f32[4]{0:T(128)S(1)}, f32[4]{0:T(128)S(1)}) all-reduce(f32[4]{0:T(128)S(1)} %dynamic-update-slice.18, f32[4]{0:T(128)S(1)} %dynamic-update-slice.22), channel_id=1, replica_groups=mesh['gz_0'=4,'gz_1'=16,'xy_0'=4,'xy_1'=2] {'xy_0'}, use_global_device_ids=true, to_apply=%add.25 | all-reduce | flops 8 | bytes 64
  462.2 1.4 dynamic-update-slice.23
  464.2 1.4 dynamic-update-slice.19
  465.6 12.2 %all-reduce.40 = (f32[2]{0:T(128)S(1)}, f32[2]{0:T(128)S(1)}) all-reduce(f32[2]{0:T(128)S(1)} %dynamic-update-slice.19, f32[2]{0:T(128)S(1)} %dynamic-update-slice.23), channel_id=1, replica_groups=mesh['gz_0'=4,'gz_1'=16,'xy_0'=4,'xy_1'=2] {'xy_1'}, use_global_device_ids=true, to_apply=%add.26 | all-reduce | flops 4 | bytes 32
  (157 shorter events, 46.4 us)
Async XLA Ops:
  1.4 37.0 %collective-permute-start.3 = (s32[4,1024]{1,0:T(4,128)S(1)}, s32[4,1024]{1,0:T(4,128)S(1)}, u32[]{:S(2)}, u32[]{:S(2)}) collective-permute-start(s32[4,1024]{1,0:T(4,128)S(1)} %broadcast_add_fusion), channel_id=1, source_target_pairs={{0,8},{8,16},{16,24},{24,32},{32,40},{40,48},{48,56},{56,64},{64,7... | collective-permute-start | bytes 49160 | tf_op jit(solution)/shard_map/ppermute | solution.py:24
  6.5 46.1 %collective-permute-start.4 = (f32[4,1024]{1,0:T(4,128)S(1)}, f32[4,1024]{1,0:T(4,128)S(1)}, u32[]{:S(2)}, u32[]{:S(2)}) collective-permute-start(f32[4,1024]{1,0:T(4,128)S(1)} %bitcast.146), channel_id=1, source_target_pairs={{0,8},{8,16},{16,24},{24,32},{32,40},{40,48},{48,56},{56,64},{64,7... | collective-permute-start | bytes 49160 | tf_op jit(solution)/shard_map/ppermute | solution.py:24
  11.1 96.8 %collective-permute-start = (f32[2,1,2048]{2,1,0:T(1,128)S(1)}, f32[2,1,2048]{2,1,0:T(1,128)S(1)}, u32[]{:S(2)}, u32[]{:S(2)}) collective-permute-start(f32[2,1,2048]{2,1,0:T(1,128)S(1)} %get-tuple-element.53), channel_id=1, source_target_pairs={{1,0},{2,1},{3,2},{4,3},{5,4},{6,5},{7,6},{9,8},{10,9},{11,10},{12... | collective-permute-start | bytes 49160 | tf_op jit(solution)/shard_map/ppermute | solution.py:37
  14.5 93.4 %collective-permute-start.2 = (f32[2,1,2048]{2,1,0:T(1,128)S(1)}, f32[2,1,2048]{2,1,0:T(1,128)S(1)}, u32[]{:S(2)}, u32[]{:S(2)}) collective-permute-start(f32[2,1,2048]{2,1,0:T(1,128)S(1)} %get-tuple-element.54), channel_id=1, source_target_pairs={{0,1},{1,2},{2,3},{3,4},{4,5},{5,6},{6,7},{8,9},{9,10},{10,11},{11... | collective-permute-start | bytes 49160 | tf_op jit(solution)/shard_map/ppermute | solution.py:35
  18.1 20.3 %collective-permute-start.1 = (f32[1,2048]{1,0:T(1,128)S(1)}, f32[1,2048]{1,0:T(1,128)S(1)}, u32[]{:S(2)}, u32[]{:S(2)}) collective-permute-start(f32[1,2048]{1,0:T(1,128)S(1)} %slice_bitcast_fusion.1), channel_id=1, source_target_pairs={{0,1},{1,2},{2,3},{3,4},{4,5},{5,6},{6,7},{8,9},{9,10},{10,11},{11... | collective-permute-start | bytes 24584 | tf_op jit(solution)/shard_map/ppermute | solution.py:24
  23.8 5.5 %copy-start.12 = (s32[1024]{0:T(1024)}, s32[1024]{0:T(1024)S(1)}, u32[]{:S(2)}) copy-start(s32[1024]{0:T(1024)S(1)} %broadcast_clamp_fusion) | copy-start | bytes 12292
  23.8 34.3 %copy-start.10 = (f32[1024]{0:T(1024)}, f32[1024]{0:T(1024)S(1)}, u32[]{:S(2)}) copy-start(f32[1024]{0:T(1024)S(1)} %fusion.35) | copy-start | bytes 12292
  23.8 14.5 %copy-start.2 = (f32[1,8,2048]{2,1,0:T(8,128)S(1)}, f32[1,8,2048]{2,1,0:T(8,128)}, u32[]{:S(2)}) copy-start(f32[1,8,2048]{2,1,0:T(8,128)} %param.10) | copy-start | bytes 196612
  53.5 4.6 collective-permute-start.5
  58.2 5.5 %collective-permute-start.6 = (f32[2,1024]{1,0:T(2,128)S(1)}, f32[2,1024]{1,0:T(2,128)S(1)}, u32[]{:S(2)}, u32[]{:S(2)}) collective-permute-start(f32[2,1024]{1,0:T(2,128)S(1)} %get-tuple-element.40), channel_id=1, source_target_pairs={{0,8},{8,16},{16,24},{24,32},{32,40},{40,48},{48,56},{56,64},{64,7... | collective-permute-start | bytes 24584 | tf_op jit(solution)/shard_map/ppermute | solution.py:24
  62.9 39.6 %copy-start.14 = (s32[5120,1]{0,1:T(1,128)}, s32[5120,1]{0,1:T(1,128)S(1)}, u32[]{:S(2)}) copy-start(s32[5120,1]{0,1:T(1,128)S(1)} %pad_add_fusion) | copy-start | bytes 61444
  63.0 155.1 %copy-start.9 = (f32[1,8,4,128]{3,1,2,0:T(8,128)}, f32[1,8,4,128]{3,1,2,0:T(8,128)S(1)}, u32[]{:S(2)}) copy-start(f32[1,8,4,128]{3,1,2,0:T(8,128)S(1)} %copy.76) | copy-start | bytes 49156
  102.6 5.3 %copy-start = (f32[2,1,8,2048]{3,2,1,0:T(8,128)S(1)}, f32[2,1,8,2048]{3,2,1,0:T(8,128)}, u32[]{:S(2)}) copy-start(f32[2,1,8,2048]{3,2,1,0:T(8,128)} %param.9) | copy-start | bytes 393220
  102.6 5.3 %copy-start.1 = (f32[1,8,2048]{2,1,0:T(8,128)S(1)}, f32[1,8,2048]{2,1,0:T(8,128)}, u32[]{:S(2)}) copy-start(f32[1,8,2048]{2,1,0:T(8,128)} %param.11) | copy-start | bytes 196612
  102.6 5.3 %copy-start.3 = (f32[1,8,2048]{2,1,0:T(8,128)S(1)}, f32[1,8,2048]{2,1,0:T(8,128)}, u32[]{:S(2)}) copy-start(f32[1,8,2048]{2,1,0:T(8,128)} %param.12) | copy-start | bytes 196612
  184.7 17.1 %copy-start.13 = (s32[1024]{0:T(1024)S(1)}, s32[1024]{0:T(1024)}, u32[]{:S(2)}) copy-start(s32[1024]{0:T(1024)} %copy-done.12) | copy-start | bytes 12292
  184.7 23.5 %copy-start.11 = (f32[1024]{0:T(1024)S(1)}, f32[1024]{0:T(1024)}, u32[]{:S(2)}) copy-start(f32[1024]{0:T(1024)} %copy-done.10) | copy-start | bytes 12292
  199.7 8.4 %collective-permute-start.9 = (f32[2,1024]{1,0:T(2,128)S(1)}, f32[2,1024]{1,0:T(2,128)S(1)}, u32[]{:S(2)}, u32[]{:S(2)}) collective-permute-start(f32[2,1024]{1,0:T(2,128)S(1)} %bitcast.148), channel_id=1, source_target_pairs={{8,0},{16,8},{24,16},{32,24},{40,32},{48,40},{56,48},{64,56},{72,6... | collective-permute-start | bytes 24584 | tf_op jit(solution)/shard_map/ppermute | solution.py:24
  208.2 9.8 %collective-permute-start.10 = (f32[2,1024]{1,0:T(2,128)S(1)}, f32[2,1024]{1,0:T(2,128)S(1)}, u32[]{:S(2)}, u32[]{:S(2)}) collective-permute-start(f32[2,1024]{1,0:T(2,128)S(1)} %get-tuple-element.37), channel_id=1, source_target_pairs={{0,8},{8,16},{16,24},{24,32},{32,40},{40,48},{48,56},{56,64},{64,7... | collective-permute-start | bytes 24584 | tf_op jit(solution)/shard_map/ppermute | solution.py:24
  212.2 50.1 %collective-permute-start.7 = (f32[2,1,2048]{2,1,0:T(1,128)S(1)}, f32[2,1,2048]{2,1,0:T(1,128)S(1)}, u32[]{:S(2)}, u32[]{:S(2)}) collective-permute-start(f32[2,1,2048]{2,1,0:T(1,128)S(1)} %get-tuple-element.49), channel_id=1, source_target_pairs={{1,0},{2,1},{3,2},{4,3},{5,4},{6,5},{7,6},{9,8},{10,9},{11,10},{12... | collective-permute-start | bytes 49160 | tf_op jit(solution)/shard_map/ppermute | solution.py:37
  215.0 47.3 %collective-permute-start.8 = (f32[2,1,2048]{2,1,0:T(1,128)S(1)}, f32[2,1,2048]{2,1,0:T(1,128)S(1)}, u32[]{:S(2)}, u32[]{:S(2)}) collective-permute-start(f32[2,1,2048]{2,1,0:T(1,128)S(1)} %get-tuple-element.50), channel_id=1, source_target_pairs={{0,1},{1,2},{2,3},{3,4},{4,5},{5,6},{6,7},{8,9},{9,10},{10,11},{11... | collective-permute-start | bytes 49160 | tf_op jit(solution)/shard_map/ppermute | solution.py:35
  257.0 5.9 %copy-start.7 = (f32[2,8,2047]{2,1,0:T(8,128)S(1)}, f32[2,8,2047]{2,1,0:T(8,128)}, u32[]{:S(2)}) copy-start(f32[2,8,2047]{2,1,0:T(8,128)} %get-tuple-element.47) | copy-start | bytes 393028
  257.0 5.9 %copy-start.8 = (f32[2,8,2047]{2,1,0:T(8,128)S(1)}, f32[2,8,2047]{2,1,0:T(8,128)}, u32[]{:S(2)}) copy-start(f32[2,8,2047]{2,1,0:T(8,128)} %get-tuple-element.48) | copy-start | bytes 393028
  262.3 0.6 copy-start.15
  262.3 0.6 copy-start.16
  349.8 8.9 %collective-permute-start.13 = (f32[2,1024]{1,0:T(2,128)S(1)}, f32[2,1024]{1,0:T(2,128)S(1)}, u32[]{:S(2)}, u32[]{:S(2)}) collective-permute-start(f32[2,1024]{1,0:T(2,128)S(1)} %bitcast.147), channel_id=1, source_target_pairs={{8,0},{16,8},{24,16},{32,24},{40,32},{48,40},{56,48},{64,56},{72,6... | collective-permute-start | bytes 24584 | tf_op jit(solution)/shard_map/ppermute | solution.py:24
  359.5 10.5 %collective-permute-start.14 = (f32[2,1024]{1,0:T(2,128)S(1)}, f32[2,1024]{1,0:T(2,128)S(1)}, u32[]{:S(2)}, u32[]{:S(2)}) collective-permute-start(f32[2,1024]{1,0:T(2,128)S(1)} %get-tuple-element.34), channel_id=1, source_target_pairs={{0,8},{8,16},{16,24},{24,32},{32,40},{40,48},{48,56},{56,64},{64,7... | collective-permute-start | bytes 24584 | tf_op jit(solution)/shard_map/ppermute | solution.py:24
  364.4 51.9 %collective-permute-start.11 = (f32[2,1,2048]{2,1,0:T(1,128)}, f32[2,1,2048]{2,1,0:T(1,128)S(1)}, u32[]{:S(2)}, u32[]{:S(2)}) collective-permute-start(f32[2,1,2048]{2,1,0:T(1,128)} %get-tuple-element.45), channel_id=1, source_target_pairs={{1,0},{2,1},{3,2},{4,3},{5,4},{6,5},{7,6},{9,8},{10,9},{11,10},{12... | collective-permute-start | bytes 49160 | tf_op jit(solution)/shard_map/ppermute | solution.py:37
  366.9 49.4 %collective-permute-start.12 = (f32[2,1,2048]{2,1,0:T(1,128)}, f32[2,1,2048]{2,1,0:T(1,128)}, u32[]{:S(2)}, u32[]{:S(2)}) collective-permute-start(f32[2,1,2048]{2,1,0:T(1,128)} %get-tuple-element.46), channel_id=1, source_target_pairs={{0,1},{1,2},{2,3},{3,4},{4,5},{5,6},{6,7},{8,9},{9,10},{10,11},{11... | collective-permute-start | bytes 49160 | tf_op jit(solution)/shard_map/ppermute | solution.py:35
  411.0 5.3 %copy-start.4 = (f32[1,8,2048]{2,1,0:T(8,128)S(1)}, f32[1,8,2048]{2,1,0:T(8,128)}, u32[]{:S(2)}) copy-start(f32[1,8,2048]{2,1,0:T(8,128)} %param.12) | copy-start | bytes 196612
  411.0 5.3 %copy-start.5 = (f32[2,8,2047]{2,1,0:T(8,128)S(1)}, f32[2,8,2047]{2,1,0:T(8,128)}, u32[]{:S(2)}) copy-start(f32[2,8,2047]{2,1,0:T(8,128)} %get-tuple-element.43) | copy-start | bytes 393028
  411.0 5.3 %copy-start.6 = (f32[2,8,2047]{2,1,0:T(8,128)S(1)}, f32[2,8,2047]{2,1,0:T(8,128)}, u32[]{:S(2)}) copy-start(f32[2,8,2047]{2,1,0:T(8,128)} %get-tuple-element.44) | copy-start | bytes 393028
